TPU v7x, 32 devices: a whole 2x2x4 slice. The times are simulated.
32 devices in a mesh: row: 4 (over z), col: 8 (over y, x, core).
Axes of the slice: x: 2, y: 2, z: 4, core: 2. Of those that a mesh axis runs over, the one named last changes fastest.
Arguments:
- inputs: bfloat16 [768, 8192], P('col', 'row'), may hold values from -6 to 6
- out_grad: bfloat16 [768, 8192], P('col', 'row'), may hold values from -1.5 to 1.5
- w_gate: bfloat16 [8192, 28672], P('row', 'col'), may hold values from -0.0625 to 0.0625
- w_up: bfloat16 [8192, 28672], P('row', 'col'), may hold values from -0.0625 to 0.0625
- w_down: bfloat16 [28672, 8192], P('col', 'row'), may hold values from -0.03125 to 0.03125
Outputs:
- grad_inputs: bfloat16 [768, 8192], P('col', 'row')
- grad_wgate: bfloat16 [8192, 28672], P('row', 'col')
- grad_wup: bfloat16 [8192, 28672], P('row', 'col')
- grad_down: bfloat16 [28672, 8192], P('col', 'row')
All inputs are finite; a program needn't handle non-finite values.
Results may differ from a plain program's by a relative error of at most 0.025.
Values may be sent and summed in bfloat16 or wider, within the bound.
A program may use at most 192 MiB of HBM per device.

v0:
```python
import jax
import jax.numpy as jnp
from jax import lax
from jax.sharding import PartitionSpec as P


def rounded(value):
    narrow = lax.optimization_barrier(value.astype(jnp.bfloat16))
    return narrow.astype(jnp.float32)


def pointwise(gate, up, grad_hidden):
    squash = jax.nn.sigmoid(gate)
    activated = gate * squash
    hidden = (activated * up).astype(jnp.bfloat16)
    grad_gate = (grad_hidden * up * squash * (1.0 + gate * (1.0 - squash))).astype(jnp.bfloat16)
    grad_upact = (grad_hidden * activated).astype(jnp.bfloat16)
    return (hidden, grad_gate, grad_upact)


def local(inputs, out_grad, w_gate, w_up, w_down):
    in_all, grad_all = (
        lax.all_gather(inputs, "col", axis=0, tiled=True),
        lax.all_gather(out_grad, "col", axis=0, tiled=True),
    )
    gate_part = rounded(jnp.dot(in_all, w_gate, preferred_element_type=jnp.float32))
    up_part = rounded(jnp.dot(in_all, w_up, preferred_element_type=jnp.float32))
    hidden_part = rounded(
        lax.dot_general(
            grad_all, w_down, (((1,), (1,)), ((), ())), preferred_element_type=jnp.float32
        )
    )
    gate, up, grad_hidden = (
        lax.psum_scatter(
            gate_part.astype(jnp.bfloat16), "row", scatter_dimension=0, tiled=True
        ).astype(jnp.float32),
        lax.psum_scatter(
            up_part.astype(jnp.bfloat16), "row", scatter_dimension=0, tiled=True
        ).astype(jnp.float32),
        lax.psum_scatter(
            hidden_part.astype(jnp.bfloat16), "row", scatter_dimension=0, tiled=True
        ).astype(jnp.float32),
    )
    hidden, grad_gate, grad_upact = pointwise(gate, up, grad_hidden)
    hidden_all, gate_grads, up_grads = (
        lax.all_gather(hidden, "row", axis=0, tiled=True),
        lax.all_gather(grad_gate, "row", axis=0, tiled=True),
        lax.all_gather(grad_upact, "row", axis=0, tiled=True),
    )
    token_contract = (((0,), (0,)), ((), ()))
    grad_down = lax.dot_general(
        hidden_all, grad_all, token_contract, preferred_element_type=jnp.float32
    ).astype(jnp.bfloat16)
    grad_wgate = lax.dot_general(
        in_all, gate_grads, token_contract, preferred_element_type=jnp.float32
    ).astype(jnp.bfloat16)
    grad_wup = lax.dot_general(
        in_all, up_grads, token_contract, preferred_element_type=jnp.float32
    ).astype(jnp.bfloat16)
    unit_contract = (((1,), (1,)), ((), ()))
    total = lax.dot_general(gate_grads, w_gate, unit_contract, preferred_element_type=jnp.float32)
    grad_inputs = lax.psum_scatter(
        (
            total
            + lax.dot_general(up_grads, w_up, unit_contract, preferred_element_type=jnp.float32)
        ).astype(jnp.bfloat16),
        "col",
        scatter_dimension=0,
        tiled=True,
    )
    return (grad_inputs, grad_wgate, grad_wup, grad_down)


def solution(mesh):
    return jax.shard_map(
        local,
        mesh=mesh,
        in_specs=(
            P("col", "row"),
            P("col", "row"),
            P("row", "col"),
            P("row", "col"),
            P("col", "row"),
        ),
        out_specs=(P("col", "row"), P("row", "col"), P("row", "col"), P("col", "row")),
        check_vma=False,
    )
```

profile of v0, /device:TPU:0, one launch (start us, length us, event | category | flops | bytes accessed | tf_op | source)
XLA Modules:
  0.0 751.6 jit_solution(15155201527250581739)
XLA Ops:
  7.2 0.7 all-gather.8.cloned.1.call-update
  7.9 0.7 all-gather.6.cloned.1.call-update
  8.7 36.2 %all-gather.8.cloned.1.call-done = bf16[768,2048]{1,0:T(8,128)(2,1)} async-done(((bf16[96,2048]{1,0:T(8,128)(2,1)}), bf16[768,2048]{1,0:T(8,128)(2,1)}) %all-gather.8.cloned.1.call-update) | async-done | bytes 3145744 | tf_op jit(solution)/shard_map/all_gather | solution.py:23
  44.9 17.2 %convolution_convert_fusion.4 = bf16[768,3584]{1,0:T(8,128)(2,1)} fusion(bf16[768,2048]{1,0:T(8,128)(2,1)} %all-gather.8.cloned.1.call-done, bf16[2048,3584]{1,0:T(8,128)(2,1)} %param.8), kind=kOutput, calls=%fused_computation.6 | convolution fusion | flops 11277041664 | bytes 23330816 | tf_op jit(solution)/shard_map/dot_general | solution.py:27
  62.2 1.8 copy-done.1
  64.0 16.3 %convolution_convert_fusion.3 = bf16[768,3584]{1,0:T(8,128)(2,1)} fusion(bf16[768,2048]{1,0:T(8,128)(2,1)S(1)} %copy-done.1, bf16[2048,3584]{1,0:T(8,128)(2,1)} %param.7), kind=kOutput, calls=%fused_computation.5 | convolution fusion | flops 11277041664 | bytes 23330816 | tf_op jit(solution)/shard_map/dot_general | solution.py:26
  80.6 17.3 %convolution_convert_fusion.5 = bf16[768,3584]{1,0:T(8,128)(2,1)} fusion(bf16[768,2048]{1,0:T(8,128)(2,1)} %all-gather.6.cloned.1.call-done, bf16[3584,2048]{1,0:T(8,128)(2,1)} %param.9), kind=kOutput, calls=%fused_computation.7 | convolution fusion | flops 11277041664 | bytes 23330816 | tf_op jit(solution)/shard_map/dot_general | solution.py:29
  98.0 82.1 %reduce-scatter.7.cloned.1.call-done = bf16[192,3584]{1,0:T(8,128)(2,1)} async-done(((bf16[768,3584]{1,0:T(8,128)(2,1)}), bf16[192,3584]{1,0:T(8,128)(2,1)}) %reduce-scatter.7.cloned.1.call-update) | async-done | bytes 1376272 | tf_op jit(solution)/shard_map/reduce_scatter | solution.py:37
  180.1 101.3 %reduce-scatter.9.cloned.1.call-done = bf16[192,3584]{1,0:T(8,128)(2,1)} async-done(((bf16[768,3584]{1,0:T(8,128)(2,1)}), bf16[192,3584]{1,0:T(8,128)(2,1)}) %reduce-scatter.9.cloned.1.call-update) | async-done | bytes 1376272 | tf_op jit(solution)/shard_map/reduce_scatter | solution.py:34
  281.4 101.3 %reduce-scatter.5.cloned.1.call-done = bf16[192,3584]{1,0:T(8,128)(2,1)} async-done(((bf16[768,3584]{1,0:T(8,128)(2,1)}), bf16[192,3584]{1,0:T(8,128)(2,1)}) %reduce-scatter.5.cloned.1.call-update) | async-done | bytes 1376272 | tf_op jit(solution)/shard_map/reduce_scatter | solution.py:40
  382.6 5.6 fusion.6
  388.3 0.7 all-gather.10.cloned.1.call-update
  389.1 0.7 all-gather.14.cloned.1.call-update
  390.0 101.3 %all-gather.12.cloned.1.call-done = bf16[768,3584]{1,0:T(8,128)(2,1)} async-done(((bf16[192,3584]{1,0:T(8,128)(2,1)}), bf16[768,3584]{1,0:T(8,128)(2,1)}) %all-gather.12.cloned.1.call-update) | async-done | bytes 5505040 | tf_op jit(solution)/shard_map/all_gather | solution.py:48
  491.3 16.7 %fusion.1 = bf16[2048,3584]{0,1:T(8,128)(2,1)} fusion(bf16[768,3584]{1,0:T(8,128)(2,1)} %all-gather.12.cloned.1.call-done, bf16[768,2048]{1,0:T(8,128)(2,1)S(1)} %copy-done.1), kind=kOutput, calls=%fused_computation.4 | convolution fusion | flops 11281629184 | bytes 23330816 | tf_op jit(solution)/shard_map/dot_general | solution.py:57
  508.0 18.7 %copy.10 = bf16[2048,3584]{1,0:T(8,128)(2,1)} copy(bf16[2048,3584]{0,1:T(8,128)(2,1)} %fusion.1) | data formatting | bytes 29360128
  526.7 67.6 %all-gather.10.cloned.1.call-done = bf16[768,3584]{1,0:T(8,128)(2,1)} async-done(((bf16[192,3584]{1,0:T(8,128)(2,1)}), bf16[768,3584]{1,0:T(8,128)(2,1)}) %all-gather.10.cloned.1.call-update) | async-done | bytes 5505040 | tf_op jit(solution)/shard_map/all_gather | solution.py:47
  594.2 18.1 %fusion.11 = f32[768,2048]{1,0:T(8,128)} fusion(bf16[768,3584]{1,0:T(8,128)(2,1)} %all-gather.10.cloned.1.call-done, bf16[2048,3584]{1,0:T(8,128)(2,1)} %param.7), kind=kOutput, calls=%fused_computation.24 | convolution fusion | flops 11274289152 | bytes 26476544 | tf_op jit(solution)/shard_map/dot_general | solution.py:61
  612.3 18.6 %add_convert_fusion = bf16[768,2048]{1,0:T(8,128)(2,1)} fusion(f32[768,2048]{1,0:T(8,128)} %fusion.11, bf16[768,3584]{1,0:T(8,128)(2,1)} %all-gather.12.cloned.1.call-done, bf16[2048,3584]{1,0:T(8,128)(2,1)} %param.8), kind=kOutput, calls=%fused_computation.8 | convolution fusion | flops 11277434880 | bytes 29622272 | tf_op jit(solution)/shard_map/dot_general | solution.py:65
  630.9 17.0 %fusion = bf16[2048,3584]{0,1:T(8,128)(2,1)} fusion(bf16[768,3584]{1,0:T(8,128)(2,1)} %all-gather.10.cloned.1.call-done, bf16[768,2048]{1,0:T(8,128)(2,1)S(1)} %copy-done.1), kind=kOutput, calls=%fused_computation.3 | convolution fusion | flops 11281629184 | bytes 23330816 | tf_op jit(solution)/shard_map/dot_general | solution.py:54
  647.9 18.8 %copy.9 = bf16[2048,3584]{1,0:T(8,128)(2,1)} copy(bf16[2048,3584]{0,1:T(8,128)(2,1)} %fusion) | data formatting | bytes 29360128
  666.7 29.8 %all-gather.14.cloned.1.call-done = bf16[768,3584]{1,0:T(8,128)(2,1)} async-done(((bf16[192,3584]{1,0:T(8,128)(2,1)}), bf16[768,3584]{1,0:T(8,128)(2,1)}) %all-gather.14.cloned.1.call-update) | async-done | bytes 5505040 | tf_op jit(solution)/shard_map/all_gather | solution.py:46
  696.6 16.7 %convolution_convert_fusion = bf16[3584,2048]{1,0:T(8,128)(2,1)} fusion(bf16[768,3584]{1,0:T(8,128)(2,1)} %all-gather.14.cloned.1.call-done, bf16[768,2048]{1,0:T(8,128)(2,1)S(1)} %copy-done), kind=kOutput, calls=%fused_computation | convolution fusion | flops 11281629184 | bytes 23330816 | tf_op jit(solution)/shard_map/dot_general | solution.py:51
  713.2 31.9 %reduce-scatter.11.cloned.1.call-done = bf16[96,2048]{1,0:T(8,128)(2,1)} async-done(((bf16[768,2048]{1,0:T(8,128)(2,1)}), bf16[96,2048]{1,0:T(8,128)(2,1)}) %reduce-scatter.11.cloned.1.call-update) | async-done | bytes 393232 | tf_op jit(solution)/shard_map/reduce_scatter | solution.py:62
  (18 shorter events, 0.9 us)
Async XLA Ops:
  7.2 37.8 %all-gather.8.cloned.1.call-start = ((), (), s32[]{:S(2)}) async-start(), calls=%async_computation.6 | async-start | bytes 3538944 | tf_op jit(solution)/shard_map/all_gather | solution.py:23
  7.9 72.7 %all-gather.6.cloned.1.call-start = ((), (), s32[]{:S(2)}) async-start(), calls=%async_computation.4 | async-start | bytes 3538944 | tf_op jit(solution)/shard_map/all_gather | solution.py:24
  8.6 171.4 %reduce-scatter.7.cloned.1.call-start = ((), (), s32[]{:S(2)}) async-start(), calls=%async_computation.7 | async-start | bytes 6881280 | tf_op jit(solution)/shard_map/reduce_scatter | solution.py:37
  62.1 1.9 copy-start.1
  62.2 219.2 %reduce-scatter.9.cloned.1.call-start = ((), (), s32[]{:S(2)}) async-start(), calls=%async_computation.8 | async-start | bytes 6881280 | tf_op jit(solution)/shard_map/reduce_scatter | solution.py:34
  80.4 302.3 %reduce-scatter.5.cloned.1.call-start = ((), (), s32[]{:S(2)}) async-start(), calls=%async_computation.5 | async-start | bytes 6881280 | tf_op jit(solution)/shard_map/reduce_scatter | solution.py:40
  97.9 393.4 %all-gather.12.cloned.1.call-start = ((), (), s32[]{:S(2)}) async-start(), calls=%async_computation.10 | async-start | bytes 6881280 | tf_op jit(solution)/shard_map/all_gather | solution.py:48
  388.3 206.0 %all-gather.10.cloned.1.call-start = ((), (), s32[]{:S(2)}) async-start(), calls=%async_computation.9 | async-start | bytes 6881280 | tf_op jit(solution)/shard_map/all_gather | solution.py:47
  389.0 307.5 %all-gather.14.cloned.1.call-start = ((), (), s32[]{:S(2)}) async-start(), calls=%async_computation.12 | async-start | bytes 6881280 | tf_op jit(solution)/shard_map/all_gather | solution.py:46
  389.8 355.3 %reduce-scatter.11.cloned.1.call-start = ((), (), s32[]{:S(2)}) async-start(), calls=%async_computation.11 | async-start | bytes 3538944 | tf_op jit(solution)/shard_map/reduce_scatter | solution.py:62
  647.9 48.7 %copy-start = (bf16[768,2048]{1,0:T(8,128)(2,1)S(1)}, bf16[768,2048]{1,0:T(8,128)(2,1)}, u32[]{:S(2)}) copy-start(bf16[768,2048]{1,0:T(8,128)(2,1)} %all-gather.6.cloned.1.call-done) | copy-start | bytes 9437188
Sparse Core Ops, SparseCore 0:
  9.9 35.0 all-gather.7
  46.8 32.3 all-gather.5
  82.0 97.9 reduce-scatter.6
  182.8 98.5 reduce-scatter.8
  284.1 98.5 reduce-scatter.4
  388.4 102.8 all-gather.11
  493.5 100.7 all-gather.9
  595.8 100.7 all-gather.13
  700.5 44.5 reduce-scatter.10
where the time goes:
time: 753 us; the launch traced here: 752 us
  waiting for transfers between devices  554 us (74%)
  matrix products  138 us (18%)
  local copies, waits for them, and re-layouts  39.3 us (5%)
  between operations  13.9 us (2%)
    all_gather x1, waiting for transfers between devices, local(): lax.all_gather(grad_upact, 'row', axis=0, tiled=True)  101 us
    reduce_scatter x1, waiting for transfers between devices, local(): lax.psum_scatter(gate_part.astype(jnp.bfloat16), 'row', scatter_dimension...  101 us
    reduce_scatter x1, waiting for transfers between devices, local(): lax.psum_scatter(hidden_part.astype(jnp.bfloat16), 'row', scatter_dimensi...  101 us
    reduce_scatter x1, waiting for transfers between devices, local(): lax.psum_scatter(up_part.astype(jnp.bfloat16), 'row', scatter_dimension=0...  82.1 us
    all_gather x1, waiting for transfers between devices, local(): lax.all_gather(grad_gate, 'row', axis=0, tiled=True)  67.6 us
    unnamed x6, local copies, waits for them, and re-layouts  39.3 us
    all_gather x1, waiting for transfers between devices, local(): lax.all_gather(inputs, 'col', axis=0, tiled=True)  36.2 us
    reduce_scatter x1, waiting for transfers between devices, local(): lax.psum_scatter((total + lax.dot_general(up_grads, w_up, unit_contract,...  31.9 us
  transfers between devices with their start and end apart: 9, of which 8 were waited for; matrix products, arithmetic and copies ran while one was open for 23% of the time, Pallas kernels for 0%

commit v1 on v0

v1 whole, which is shorter than its diff:
```python
import functools

import jax
import jax.numpy as jnp
from jax import lax
from jax.experimental import pallas as pl
from jax.experimental.pallas import tpu as pltpu
from jax.sharding import PartitionSpec as P

BF = jnp.bfloat16
F32 = jnp.float32
UNIT = (((1,), (1,)), ((), ()))
TOKEN = (((0,), (0,)), ((), ()))
ANY = pl.BlockSpec(memory_space=pl.ANY)
VMEM_LIMIT = 40 * 1024 * 1024


def divisor(size, *tries):
    for width in tries:
        if size % width == 0:
            return width
    return size


def call(body, grid, in_specs, out_specs, out_shape, cost, aliases=None):
    return pl.pallas_call(
        body,
        grid=grid,
        in_specs=in_specs,
        out_specs=out_specs,
        out_shape=out_shape,
        input_output_aliases=aliases or {},
        cost_estimate=pl.CostEstimate(flops=cost[0], bytes_accessed=cost[1], transcendentals=0),
        compiler_params=pltpu.CompilerParams(vmem_limit_bytes=VMEM_LIMIT),
    )


def first_body(in_ref, grad_ref, wg_ref, wu_ref, wd_ref, *rest):
    out_ref = rest[-1]
    x = in_ref[...]
    out_ref[0] = jnp.dot(x, wg_ref[...], preferred_element_type=F32).astype(BF)
    out_ref[1] = jnp.dot(x, wu_ref[...], preferred_element_type=F32).astype(BF)
    out_ref[2] = lax.dot_general(
        grad_ref[...], wd_ref[...], UNIT, preferred_element_type=F32
    ).astype(BF)


def add_body(mine_ref, got_ref, dep_ref, out_ref):
    out_ref[...] = (mine_ref[...].astype(F32) + got_ref[...].astype(F32)).astype(BF)


def pointwise_body(mine_ref, got_ref, dep_ref, out_ref):
    gate = mine_ref[0].astype(F32) + got_ref[0].astype(F32)
    up = mine_ref[1].astype(F32) + got_ref[1].astype(F32)
    grad_hidden = mine_ref[2].astype(F32) + got_ref[2].astype(F32)
    squash = jax.nn.sigmoid(gate)
    activated = gate * squash
    out_ref[0] = (activated * up).astype(BF)
    out_ref[1] = (grad_hidden * up * squash * (1.0 + gate * (1.0 - squash))).astype(BF)
    out_ref[2] = (grad_hidden * activated).astype(BF)


def select_body(low, high, mine_ref, got_ref, dep_ref, out_ref):
    rank = lax.axis_index("row")
    take = (rank == low) | (rank == high)

    @pl.when(take)
    def _():
        out_ref[...] = got_ref[...]

    @pl.when(jnp.logical_not(take))
    def _():
        out_ref[...] = mine_ref[...]


def second_body(low, high, fresh, *refs):
    mine_ref, got_ref, inT_ref, grad_ref, wg_ref, wu_ref = refs[:6]
    total_in = None if fresh else refs[6]
    total_ref, gw_ref, gu_ref, gd_ref = refs[-4:]
    rank = lax.axis_index("row")
    take = (rank == low) | (rank == high)

    def run(src):
        total = lax.dot_general(src[1], wg_ref[...], UNIT, preferred_element_type=F32)
        total = total + lax.dot_general(src[2], wu_ref[...], UNIT, preferred_element_type=F32)
        total_ref[...] = total if fresh else total_in[...] + total
        gw_ref[...] = jnp.dot(inT_ref[...], src[1], preferred_element_type=F32).astype(BF)
        gu_ref[...] = jnp.dot(inT_ref[...], src[2], preferred_element_type=F32).astype(BF)
        gd_ref[...] = lax.dot_general(
            src[0], grad_ref[...], TOKEN, preferred_element_type=F32
        ).astype(BF)

    @pl.when(take)
    def _():
        run(got_ref)

    @pl.when(jnp.logical_not(take))
    def _():
        run(mine_ref)


def local(n, inputs, out_grad, w_gate, w_up, w_down):
    half = n // 2
    model, units = w_gate.shape
    width = divisor(units, 256, 128)
    count = units // width
    in_all = lax.all_gather(inputs, "col", axis=0, tiled=True)
    grad_all = lax.all_gather(out_grad, "col", axis=0, tiled=True)
    in_T = in_all.T
    tokens = in_all.shape[0]
    rows = divisor(tokens, 384, 256, 128)
    depth = divisor(model, 512, 256, 128)
    pack = jax.ShapeDtypeStruct((3, tokens, width), BF)
    macs = tokens * width * model
    slab = tokens * width * 6

    perms = []
    for s in range(half - 1):
        perms.append([(s, s + 1), (n - 1 - s, n - 2 - s)])
    perms.append([(half - 1, half), (half, half - 1)])
    for s in range(half - 1):
        perms.append([(half - 1 - s, half - 2 - s), (half + s, half + s + 1)])

    def first(k, dep):
        deps = [] if dep is None else [dep]
        return call(
            first_body,
            (tokens // rows,),
            [
                pl.BlockSpec((rows, model), lambda i: (i, 0)),
                pl.BlockSpec((rows, model), lambda i: (i, 0)),
                pl.BlockSpec((model, width), lambda i: (0, k)),
                pl.BlockSpec((model, width), lambda i: (0, k)),
                pl.BlockSpec((width, model), lambda i: (k, 0)),
            ]
            + [ANY] * len(deps),
            pl.BlockSpec((3, rows, width), lambda i: (0, i, 0)),
            pack,
            (6 * macs, tokens * model * 4 + 6 * model * width + slab),
        )(in_all, grad_all, w_gate, w_up, w_down, *deps)

    def combine(j, mine, got, dep):
        if j < half - 1:
            body = add_body
        elif j == half - 1:
            body = pointwise_body
        else:
            s = j - half
            body = functools.partial(select_body, half - 2 - s, half + s + 1)
        spec = pl.BlockSpec((3, rows // 2, width), lambda i: (0, i, 0))
        return call(
            body, (tokens // rows * 2,), [spec, spec, ANY], spec, pack, (10 * slab, 3 * slab)
        )(mine, got, dep)

    def second(k, mine, got, state, dep):
        s = half - 2
        low, high = (half - 2 - s, half + s + 1) if half > 1 else (-1, -1)
        fresh = state is None
        whole = pl.BlockSpec((3, tokens, width), lambda i: (0, 0, 0))
        column = pl.BlockSpec((depth, width), lambda i: (i, k))
        acc = pl.BlockSpec((tokens, depth), lambda i: (0, i))
        ins = [mine, got, in_T, grad_all, w_gate, w_up]
        specs = [whole, whole, pl.BlockSpec((depth, tokens), lambda i: (i, 0)), acc, column, column]
        aliases = {}
        if not fresh:
            ins += list(state)
            specs += [acc, ANY, ANY, ANY]
            aliases = {6: 0, 7: 1, 8: 2, 9: 3}
        ins.append(dep)
        specs.append(ANY)
        return call(
            functools.partial(second_body, low, high, fresh),
            (model // depth,),
            specs,
            [acc, column, column, pl.BlockSpec((width, depth), lambda i: (k, i))],
            [
                jax.ShapeDtypeStruct((tokens, model), F32),
                jax.ShapeDtypeStruct(w_gate.shape, BF),
                jax.ShapeDtypeStruct(w_up.shape, BF),
                jax.ShapeDtypeStruct(w_down.shape, BF),
            ],
            (10 * macs, tokens * model * 12 + 10 * model * width + 2 * slab),
            aliases,
        )(*ins)

    mine, got, state, last = {}, {}, None, None
    for t in range(count + n - 1):
        if t < count:
            last = mine[t] = first(t, last)
            got[t] = lax.ppermute(mine[t], "row", perms[0])
        for j in range(n - 1):
            c = t - 1 - j
            if not 0 <= c < count:
                continue
            if j < n - 2:
                last = mine[c] = combine(j, mine[c], got[c], last)
                got[c] = lax.ppermute(mine[c], "row", perms[j + 1])
            else:
                state = second(c, mine.pop(c), got.pop(c), state, last)
                last = state[3]
    total, gw, gu, gd = state
    grad_inputs = lax.psum_scatter(total.astype(BF), "col", scatter_dimension=0, tiled=True)
    return grad_inputs, gw, gu, gd


def solution(mesh):
    return jax.shard_map(
        functools.partial(local, mesh.shape["row"]),
        mesh=mesh,
        in_specs=(P("col", "row"), P("col", "row"), P("row", "col"), P("row", "col"), P("col", "row")),
        out_specs=(P("col", "row"), P("row", "col"), P("row", "col"), P("col", "row")),
        check_vma=False,
    )
```

time: 753 us -> 592 us (0.79); the launches traced: 752 us -> 581 us
  waiting for transfers between devices: 554 us -> 230 us
  Pallas kernels: 0 us -> 231 us
  matrix products: 138 us -> 0 us
  starting transfers between devices: 0.76 us -> 76.4 us
  local copies, waits for them, and re-layouts: 39.3 us -> 24.2 us
    reduce_scatter x4 -> x1, waiting for transfers between devices: 317 us -> 43.6 us  [local(): lax.psum_scatter(total.astype(BF), 'col', scatter_dimension=0, tiled=True)]
    pallas_call x0 -> x56, Pallas kernels: none -> 231 us  [the longest x14 135 us: second(): call(functools.partial(second_body, low, high, fresh), (model // depth,),...]
    all_gather x5 -> x2, waiting for transfers between devices: 235 us -> 70.5 us  [the longest x1 36.2 us: local(): in_all = lax.all_gather(inputs, 'col', axis=0, tiled=True)]
    dot_general x8 -> x0, matrix products: 138 us -> none  [the longest x1 18.6 us: local(): lax.dot_general(up_grads, w_up, unit_contract, preferred_element_type=jnp...]
    ppermute x0 -> x42, waiting for transfers between devices: none -> 114 us  [the longest x28 65.1 us: local(): got[c] = lax.ppermute(mine[c], 'row', perms[j + 1])]
    ppermute x0 -> x42, starting transfers between devices: none -> 76.3 us  [the longest x14 45.7 us: local(): got[t] = lax.ppermute(mine[t], 'row', perms[0])]
    unnamed x6 -> x33, local copies, waits for them, and re-layouts: 39.3 us -> 19.6 us
  transfers between devices with their start and end apart: 9 -> 45, of which waited for: 8 -> 26; matrix products, arithmetic and copies ran while one was open for 23% -> 3% of each run, Pallas kernels for 0% -> 37%
where the time goes in v1:
time: 592 us; the launch traced here: 581 us
  Pallas kernels  231 us (39%)
  waiting for transfers between devices  230 us (39%)
  starting transfers between devices  76.4 us (13%)
  local copies, waits for them, and re-layouts  24.2 us (4%)
  between operations  15.1 us (3%)
    pallas_call x14, Pallas kernels, second(): call(functools.partial(second_body, low, high, fresh), (model // depth,),...  135 us
    pallas_call x14, Pallas kernels, first(): call(first_body, (tokens // rows,), [pl.BlockSpec((rows, model), lambda i...  67.5 us
    ppermute x28, waiting for transfers between devices, local(): got[c] = lax.ppermute(mine[c], 'row', perms[j + 1])  65.1 us
    ppermute x14, waiting for transfers between devices, local(): got[t] = lax.ppermute(mine[t], 'row', perms[0])  49.2 us
    ppermute x14, starting transfers between devices, local(): got[t] = lax.ppermute(mine[t], 'row', perms[0])  45.7 us
    reduce_scatter x1, waiting for transfers between devices, local(): lax.psum_scatter(total.astype(BF), 'col', scatter_dimension=0, tiled=True)  43.6 us
    all_gather x1, waiting for transfers between devices, local(): in_all = lax.all_gather(inputs, 'col', axis=0, tiled=True)  36.2 us
    all_gather x1, waiting for transfers between devices, local(): grad_all = lax.all_gather(out_grad, 'col', axis=0, tiled=True)  34.2 us
  transfers between devices with their start and end apart: 45, of which 26 were waited for; matrix products, arithmetic and copies ran while one was open for 3% of the time, Pallas kernels for 37%

profile of v1, /device:TPU:0, one launch (start us, length us, event | category | flops | bytes accessed | tf_op | source)
XLA Modules:
  0.0 581.4 jit_solution(17576027295023288758)
XLA Ops:
  8.7 36.2 %all-gather.3.cloned.1.call-done.in_ref = bf16[768,2048]{1,0:T(8,128)(2,1)} async-done(((bf16[96,2048]{1,0:T(8,128)(2,1)}), bf16[768,2048]{1,0:T(8,128)(2,1)}) %all-gather.3.cloned.1.call-update) | async-done | bytes 3145744 | tf_op jit(solution)/shard_map/all_gather | solution.py:107
  44.9 34.2 %all-gather.5.cloned.1.call-done.grad_ref.refs_3_ = bf16[768,2048]{1,0:T(8,128)(2,1)} async-done(((bf16[96,2048]{1,0:T(8,128)(2,1)}), bf16[768,2048]{1,0:T(8,128)(2,1)}) %all-gather.5.cloned.1.call-update) | async-done | bytes 3145744 | tf_op jit(solution)/shard_map/all_gather | solution.py:108
  97.5 19.9 %collective-permute-done.1.got_ref = bf16[3,768,256]{2,1,0:T(8,128)(2,1)S(1)} collective-permute-done((bf16[3,768,256]{2,1,0:T(8,128)(2,1)S(1)}, bf16[3,768,256]{2,1,0:T(8,128)(2,1)S(1)}, u32[]{:S(2)}, u32[]{:S(2)}) %collective-permute-start.1) | collective-permute-done | bytes 1179680 | tf_op jit(solution)/shard_map/ppermute | solution.py:190
  130.8 11.9 %collective-permute-done.got_ref = bf16[3,768,256]{2,1,0:T(8,128)(2,1)S(1)} collective-permute-done((bf16[3,768,256]{2,1,0:T(8,128)(2,1)S(1)}, bf16[3,768,256]{2,1,0:T(8,128)(2,1)S(1)}, u32[]{:S(2)}, u32[]{:S(2)}) %collective-permute-start) | collective-permute-done | bytes 1179680 | tf_op jit(solution)/shard_map/ppermute | solution.py:190
  153.0 9.1 %collective-permute-start.8 = (bf16[3,768,256]{2,1,0:T(8,128)(2,1)}, bf16[3,768,256]{2,1,0:T(8,128)(2,1)}, u32[]{:S(2)}, u32[]{:S(2)}) collective-permute-start(bf16[3,768,256]{2,1,0:T(8,128)(2,1)} %shard_map.90.dep_ref.mine_ref), channel_id=1, source_target_pairs={{0,8},{24,16},{1,9},{25,17},{2,10},{26,18},{3,11},{27,19},{4,12},{... | collective-permute-start | bytes 3538952 | tf_op jit(solution)/shard_map/ppermute | solution.py:190
  181.4 8.8 %shard_map.93 = (f32[768,2048]{1,0:T(8,128)}, bf16[2048,3584]{1,0:T(8,128)(2,1)}, bf16[2048,3584]{1,0:T(8,128)(2,1)}, bf16[3584,2048]{1,0:T(8,128)(2,1)}) custom-call(bf16[3,768,256]{2,1,0:T(8,128)(2,1)} %shard_map.89.rest_0_.refs_0_, bf16[3,768,256]{2,1,0:T(8,128)(2,1)} %collective-permute-done.6.refs_1_, bf16[2048,768]{1,0:T(8,128)(2,1)S(1)} %bitcast.1, ...), custom_call_target="tpu_custom_call" | custom-call | flops 4026531840 | bytes 26476544 | tf_op jit(solution)/shard_map/pallas_call | solution.py:171
  195.0 7.2 %collective-permute-start.12 = (bf16[3,768,256]{2,1,0:T(8,128)(2,1)S(1)}, bf16[3,768,256]{2,1,0:T(8,128)(2,1)S(1)}, u32[]{:S(2)}, u32[]{:S(2)}) collective-permute-start(bf16[3,768,256]{2,1,0:T(8,128)(2,1)S(1)} %shard_map.94.dep_ref.mine_ref), channel_id=1, source_target_pairs={{0,8},{24,16},{1,9},{25,17},{2,10},{26,18},{3,11},{27,19},{4,12},{... | collective-permute-start | bytes 3538952 | tf_op jit(solution)/shard_map/ppermute | solution.py:190
  210.2 10.4 %shard_map.97 = (f32[768,2048]{1,0:T(8,128)}, bf16[2048,3584]{1,0:T(8,128)(2,1)}, bf16[2048,3584]{1,0:T(8,128)(2,1)}, bf16[3584,2048]{1,0:T(8,128)(2,1)}) custom-call(bf16[3,768,256]{2,1,0:T(8,128)(2,1)} %shard_map.92.refs_6_.refs_0_, ...), custom_call_target="tpu_custom_call", output_to_operand_aliasing={{0}: (6, {}), {1}: (7, {}), {2}: (8, {}), {3}: (9, {})} | custom-call | flops 4026531840 | bytes 26476544 | tf_op jit(solution)/shard_map/pallas_call | solution.py:171
  238.2 9.6 %shard_map.101 = (f32[768,2048]{1,0:T(8,128)}, bf16[2048,3584]{1,0:T(8,128)(2,1)}, bf16[2048,3584]{1,0:T(8,128)(2,1)}, bf16[3584,2048]{1,0:T(8,128)(2,1)}) custom-call(bf16[3,768,256]{2,1,0:T(8,128)(2,1)S(1)} %shard_map.96.refs_10_.refs_0_, ...), custom_call_target="tpu_custom_call", output_to_operand_aliasing={{0}: (6, {}), {1}: (7, {}), {2}: (8, {}), {3}: (9, {})} | custom-call | flops 4026531840 | bytes 26476544 | tf_op jit(solution)/shard_map/pallas_call | solution.py:171
  263.5 9.6 %shard_map.105 = (f32[768,2048]{1,0:T(8,128)}, bf16[2048,3584]{1,0:T(8,128)(2,1)}, bf16[2048,3584]{1,0:T(8,128)(2,1)}, bf16[3584,2048]{1,0:T(8,128)(2,1)}) custom-call(bf16[3,768,256]{2,1,0:T(8,128)(2,1)S(1)} %shard_map.100.refs_10_.refs_0_, ...), custom_call_target="tpu_custom_call", output_to_operand_aliasing={{0}: (6, {}), {1}: (7, {}), {2}: (8, {}), {3}: (9, {})} | custom-call | flops 4026531840 | bytes 26476544 | tf_op jit(solution)/shard_map/pallas_call | solution.py:171
  289.8 9.6 %shard_map.109 = (f32[768,2048]{1,0:T(8,128)}, bf16[2048,3584]{1,0:T(8,128)(2,1)}, bf16[2048,3584]{1,0:T(8,128)(2,1)}, bf16[3584,2048]{1,0:T(8,128)(2,1)}) custom-call(bf16[3,768,256]{2,1,0:T(8,128)(2,1)S(1)} %shard_map.104.refs_10_.refs_0_, ...), custom_call_target="tpu_custom_call", output_to_operand_aliasing={{0}: (6, {}), {1}: (7, {}), {2}: (8, {}), {3}: (9, {})} | custom-call | flops 4026531840 | bytes 26476544 | tf_op jit(solution)/shard_map/pallas_call | solution.py:171
  315.5 9.6 %shard_map.113 = (f32[768,2048]{1,0:T(8,128)}, bf16[2048,3584]{1,0:T(8,128)(2,1)}, bf16[2048,3584]{1,0:T(8,128)(2,1)}, bf16[3584,2048]{1,0:T(8,128)(2,1)}) custom-call(bf16[3,768,256]{2,1,0:T(8,128)(2,1)S(1)} %shard_map.108.refs_10_.refs_0_, ...), custom_call_target="tpu_custom_call", output_to_operand_aliasing={{0}: (6, {}), {1}: (7, {}), {2}: (8, {}), {3}: (9, {})} | custom-call | flops 4026531840 | bytes 26476544 | tf_op jit(solution)/shard_map/pallas_call | solution.py:171
  340.7 9.7 %shard_map.117 = (f32[768,2048]{1,0:T(8,128)}, bf16[2048,3584]{1,0:T(8,128)(2,1)}, bf16[2048,3584]{1,0:T(8,128)(2,1)}, bf16[3584,2048]{1,0:T(8,128)(2,1)}) custom-call(bf16[3,768,256]{2,1,0:T(8,128)(2,1)S(1)} %shard_map.112.refs_10_.refs_0_, ...), custom_call_target="tpu_custom_call", output_to_operand_aliasing={{0}: (6, {}), {1}: (7, {}), {2}: (8, {}), {3}: (9, {})} | custom-call | flops 4026531840 | bytes 26476544 | tf_op jit(solution)/shard_map/pallas_call | solution.py:171
  366.3 9.6 %shard_map.121 = (f32[768,2048]{1,0:T(8,128)}, bf16[2048,3584]{1,0:T(8,128)(2,1)}, bf16[2048,3584]{1,0:T(8,128)(2,1)}, bf16[3584,2048]{1,0:T(8,128)(2,1)}) custom-call(bf16[3,768,256]{2,1,0:T(8,128)(2,1)S(1)} %shard_map.116.refs_10_.refs_0_, ...), custom_call_target="tpu_custom_call", output_to_operand_aliasing={{0}: (6, {}), {1}: (7, {}), {2}: (8, {}), {3}: (9, {})} | custom-call | flops 4026531840 | bytes 26476544 | tf_op jit(solution)/shard_map/pallas_call | solution.py:171
  391.6 9.6 %shard_map.125 = (f32[768,2048]{1,0:T(8,128)}, bf16[2048,3584]{1,0:T(8,128)(2,1)}, bf16[2048,3584]{1,0:T(8,128)(2,1)}, bf16[3584,2048]{1,0:T(8,128)(2,1)}) custom-call(bf16[3,768,256]{2,1,0:T(8,128)(2,1)S(1)} %shard_map.120.refs_10_.refs_0_, ...), custom_call_target="tpu_custom_call", output_to_operand_aliasing={{0}: (6, {}), {1}: (7, {}), {2}: (8, {}), {3}: (9, {})} | custom-call | flops 4026531840 | bytes 26476544 | tf_op jit(solution)/shard_map/pallas_call | solution.py:171
  417.1 9.6 %shard_map.129 = (f32[768,2048]{1,0:T(8,128)}, bf16[2048,3584]{1,0:T(8,128)(2,1)}, bf16[2048,3584]{1,0:T(8,128)(2,1)}, bf16[3584,2048]{1,0:T(8,128)(2,1)}) custom-call(bf16[3,768,256]{2,1,0:T(8,128)(2,1)S(1)} %shard_map.124.refs_10_.refs_0_, ...), custom_call_target="tpu_custom_call", output_to_operand_aliasing={{0}: (6, {}), {1}: (7, {}), {2}: (8, {}), {3}: (9, {})} | custom-call | flops 4026531840 | bytes 26476544 | tf_op jit(solution)/shard_map/pallas_call | solution.py:171
  442.5 9.6 %shard_map.133 = (f32[768,2048]{1,0:T(8,128)}, bf16[2048,3584]{1,0:T(8,128)(2,1)}, bf16[2048,3584]{1,0:T(8,128)(2,1)}, bf16[3584,2048]{1,0:T(8,128)(2,1)}) custom-call(bf16[3,768,256]{2,1,0:T(8,128)(2,1)S(1)} %shard_map.128.refs_10_.refs_0_, ...), custom_call_target="tpu_custom_call", output_to_operand_aliasing={{0}: (6, {}), {1}: (7, {}), {2}: (8, {}), {3}: (9, {})} | custom-call | flops 4026531840 | bytes 26476544 | tf_op jit(solution)/shard_map/pallas_call | solution.py:171
  459.1 8.8 %collective-permute-done.38.refs_1_ = bf16[3,768,256]{2,1,0:T(8,128)(2,1)S(1)} collective-permute-done((bf16[3,768,256]{2,1,0:T(8,128)(2,1)S(1)}, bf16[3,768,256]{2,1,0:T(8,128)(2,1)S(1)}, u32[]{:S(2)}, u32[]{:S(2)}) %collective-permute-start.38) | collective-permute-done | bytes 1179680 | tf_op jit(solution)/shard_map/ppermute | solution.py:197
  467.9 9.6 %shard_map.136 = (f32[768,2048]{1,0:T(8,128)}, bf16[2048,3584]{1,0:T(8,128)(2,1)}, bf16[2048,3584]{1,0:T(8,128)(2,1)}, bf16[3584,2048]{1,0:T(8,128)(2,1)}) custom-call(bf16[3,768,256]{2,1,0:T(8,128)(2,1)S(1)} %shard_map.132.refs_10_.refs_0_, ...), custom_call_target="tpu_custom_call", output_to_operand_aliasing={{0}: (6, {}), {1}: (7, {}), {2}: (8, {}), {3}: (9, {})} | custom-call | flops 4026531840 | bytes 26476544 | tf_op jit(solution)/shard_map/pallas_call | solution.py:171
  479.8 13.4 %collective-permute-done.41.refs_1_ = bf16[3,768,256]{2,1,0:T(8,128)(2,1)S(1)} collective-permute-done((bf16[3,768,256]{2,1,0:T(8,128)(2,1)S(1)}, bf16[3,768,256]{2,1,0:T(8,128)(2,1)S(1)}, u32[]{:S(2)}, u32[]{:S(2)}) %collective-permute-start.41) | collective-permute-done | bytes 1179680 | tf_op jit(solution)/shard_map/ppermute | solution.py:197
  493.2 9.6 %shard_map.138 = (f32[768,2048]{1,0:T(8,128)}, bf16[2048,3584]{1,0:T(8,128)(2,1)}, bf16[2048,3584]{1,0:T(8,128)(2,1)}, bf16[3584,2048]{1,0:T(8,128)(2,1)}) custom-call(bf16[3,768,256]{2,1,0:T(8,128)(2,1)S(1)} %shard_map.135.refs_10_.refs_0_, ...), custom_call_target="tpu_custom_call", output_to_operand_aliasing={{0}: (6, {}), {1}: (7, {}), {2}: (8, {}), {3}: (9, {})} | custom-call | flops 4026531840 | bytes 26476544 | tf_op jit(solution)/shard_map/pallas_call | solution.py:171
  502.8 13.5 %copy.128.refs_9_ = bf16[3584,2048]{1,0:T(8,128)(2,1)} copy(bf16[3584,2048]{1,0:T(8,128)(2,1)} %get-tuple-element.111.refs_10_) | data formatting | bytes 29360128
  516.3 9.6 %shard_map.139 = (f32[768,2048]{1,0:T(8,128)}, bf16[2048,3584]{1,0:T(8,128)(2,1)}, bf16[2048,3584]{1,0:T(8,128)(2,1)}, bf16[3584,2048]{1,0:T(8,128)(2,1)}) custom-call(bf16[3,768,256]{2,1,0:T(8,128)(2,1)S(1)} %shard_map.137.refs_10_.refs_0_, ...), custom_call_target="tpu_custom_call", output_to_operand_aliasing={{0}: (6, {}), {1}: (7, {}), {2}: (8, {}), {3}: (9, {})} | custom-call | flops 4026531840 | bytes 26476544 | tf_op jit(solution)/shard_map/pallas_call | solution.py:171
  530.8 43.6 %reduce-scatter.2.cloned.1.call-done = bf16[96,2048]{1,0:T(8,128)(2,1)} async-done(((bf16[768,2048]{1,0:T(8,128)(2,1)}), bf16[96,2048]{1,0:T(8,128)(2,1)}) %reduce-scatter.2.cloned.1.call-update) | async-done | bytes 393232 | tf_op jit(solution)/shard_map/reduce_scatter | solution.py:202
  (160 shorter events, 233.9 us)
Async XLA Ops:
  7.2 37.8 %all-gather.3.cloned.1.call-start = ((), (), s32[]{:S(2)}) async-start(), calls=%async_computation.1 | async-start | bytes 3538944 | tf_op jit(solution)/shard_map/all_gather | solution.py:107
  7.9 71.3 %all-gather.5.cloned.1.call-start = ((), (), s32[]{:S(2)}) async-start(), calls=%async_computation.2 | async-start | bytes 3538944 | tf_op jit(solution)/shard_map/all_gather | solution.py:108
  8.6 565.8 %reduce-scatter.2.cloned.1.call-start = ((), (), s32[]{:S(2)}) async-start(), calls=%async_computation.3 | async-start | bytes 3538944 | tf_op jit(solution)/shard_map/reduce_scatter | solution.py:202
  87.7 29.7 %collective-permute-start.1 = (bf16[3,768,256]{2,1,0:T(8,128)(2,1)S(1)}, bf16[3,768,256]{2,1,0:T(8,128)(2,1)S(1)}, u32[]{:S(2)}, u32[]{:S(2)}) collective-permute-start(bf16[3,768,256]{2,1,0:T(8,128)(2,1)S(1)} %shard_map.84.rest_0_.mine_ref), channel_id=1, source_target_pairs={{0,8},{24,16},{1,9},{25,17},{2,10},{26,18},{3,11},{27,19},{4,12},{... | collective-permute-start | bytes 3538952 | tf_op jit(solution)/shard_map/ppermute | solution.py:190
  96.1 46.6 %collective-permute-start = (bf16[3,768,256]{2,1,0:T(8,128)(2,1)S(1)}, bf16[3,768,256]{2,1,0:T(8,128)(2,1)S(1)}, u32[]{:S(2)}, u32[]{:S(2)}) collective-permute-start(bf16[3,768,256]{2,1,0:T(8,128)(2,1)S(1)} %shard_map.85.dep_ref.mine_ref), channel_id=1, source_target_pairs={{0,8},{24,16},{1,9},{25,17},{2,10},{26,18},{3,11},{27,19},{4,12},{... | collective-permute-start | bytes 3538952 | tf_op jit(solution)/shard_map/ppermute | solution.py:190
  124.0 43.9 %collective-permute-start.3 = (bf16[3,768,256]{2,1,0:T(8,128)(2,1)S(1)}, bf16[3,768,256]{2,1,0:T(8,128)(2,1)S(1)}, u32[]{:S(2)}, u32[]{:S(2)}) collective-permute-start(bf16[3,768,256]{2,1,0:T(8,128)(2,1)S(1)} %shard_map.87.dep_ref.mine_ref), channel_id=1, source_target_pairs={{0,8},{24,16},{1,9},{25,17},{2,10},{26,18},{3,11},{27,19},{4,12},{... | collective-permute-start | bytes 3538952 | tf_op jit(solution)/shard_map/ppermute | solution.py:190
  146.1 33.4 %collective-permute-start.6 = (bf16[3,768,256]{2,1,0:T(8,128)(2,1)}, bf16[3,768,256]{2,1,0:T(8,128)(2,1)}, u32[]{:S(2)}, u32[]{:S(2)}) collective-permute-start(bf16[3,768,256]{2,1,0:T(8,128)(2,1)} %shard_map.89.rest_0_.refs_0_), channel_id=1, source_target_pairs={{8,0},{16,24},{9,1},{17,25},{10,2},{18,26},{11,3},{19,27},{12,4},{... | collective-permute-start | bytes 3538952 | tf_op jit(solution)/shard_map/ppermute | solution.py:197
  153.0 49.2 %collective-permute-start.8 = (bf16[3,768,256]{2,1,0:T(8,128)(2,1)}, bf16[3,768,256]{2,1,0:T(8,128)(2,1)}, u32[]{:S(2)}, u32[]{:S(2)}) collective-permute-start(bf16[3,768,256]{2,1,0:T(8,128)(2,1)} %shard_map.90.dep_ref.mine_ref), channel_id=1, source_target_pairs={{0,8},{24,16},{1,9},{25,17},{2,10},{26,18},{3,11},{27,19},{4,12},{... | collective-permute-start | bytes 3538952 | tf_op jit(solution)/shard_map/ppermute | solution.py:190
  169.8 35.7 %collective-permute-start.7 = (bf16[3,768,256]{2,1,0:T(8,128)(2,1)}, bf16[3,768,256]{2,1,0:T(8,128)(2,1)}, u32[]{:S(2)}, u32[]{:S(2)}) collective-permute-start(bf16[3,768,256]{2,1,0:T(8,128)(2,1)} %shard_map.91.dep_ref.mine_ref), channel_id=1, source_target_pairs={{8,16},{16,8},{9,17},{17,9},{10,18},{18,10},{11,19},{19,11},{12,20... | collective-permute-start | bytes 3538952 | tf_op jit(solution)/shard_map/ppermute | solution.py:197
  173.6 36.6 %collective-permute-start.5 = (bf16[3,768,256]{2,1,0:T(8,128)(2,1)}, bf16[3,768,256]{2,1,0:T(8,128)(2,1)}, u32[]{:S(2)}, u32[]{:S(2)}) collective-permute-start(bf16[3,768,256]{2,1,0:T(8,128)(2,1)} %shard_map.92.refs_6_.refs_0_), channel_id=1, source_target_pairs={{8,0},{16,24},{9,1},{17,25},{10,2},{18,26},{11,3},{19,27},{12,4},{... | collective-permute-start | bytes 3538952 | tf_op jit(solution)/shard_map/ppermute | solution.py:197
  195.0 35.0 %collective-permute-start.12 = (bf16[3,768,256]{2,1,0:T(8,128)(2,1)S(1)}, bf16[3,768,256]{2,1,0:T(8,128)(2,1)S(1)}, u32[]{:S(2)}, u32[]{:S(2)}) collective-permute-start(bf16[3,768,256]{2,1,0:T(8,128)(2,1)S(1)} %shard_map.94.dep_ref.mine_ref), channel_id=1, source_target_pairs={{0,8},{24,16},{1,9},{25,17},{2,10},{26,18},{3,11},{27,19},{4,12},{... | collective-permute-start | bytes 3538952 | tf_op jit(solution)/shard_map/ppermute | solution.py:190
  208.4 29.8 %collective-permute-start.10 = (bf16[3,768,256]{2,1,0:T(8,128)(2,1)S(1)}, bf16[3,768,256]{2,1,0:T(8,128)(2,1)S(1)}, u32[]{:S(2)}, u32[]{:S(2)}) collective-permute-start(bf16[3,768,256]{2,1,0:T(8,128)(2,1)S(1)} %shard_map.96.refs_10_.refs_0_), channel_id=1, source_target_pairs={{8,0},{16,24},{9,1},{17,25},{10,2},{18,26},{11,3},{19,27},{12,4},{... | collective-permute-start | bytes 3538952 | tf_op jit(solution)/shard_map/ppermute | solution.py:197
  225.3 30.9 %collective-permute-start.9 = (bf16[3,768,256]{2,1,0:T(8,128)(2,1)S(1)}, bf16[3,768,256]{2,1,0:T(8,128)(2,1)S(1)}, u32[]{:S(2)}, u32[]{:S(2)}) collective-permute-start(bf16[3,768,256]{2,1,0:T(8,128)(2,1)S(1)} %shard_map.98.dep_ref.mine_ref), channel_id=1, source_target_pairs={{0,8},{24,16},{1,9},{25,17},{2,10},{26,18},{3,11},{27,19},{4,12},{... | collective-permute-start | bytes 3538952 | tf_op jit(solution)/shard_map/ppermute | solution.py:190
  232.3 31.2 %collective-permute-start.15 = (bf16[3,768,256]{2,1,0:T(8,128)(2,1)S(1)}, bf16[3,768,256]{2,1,0:T(8,128)(2,1)S(1)}, u32[]{:S(2)}, u32[]{:S(2)}) collective-permute-start(bf16[3,768,256]{2,1,0:T(8,128)(2,1)S(1)} %shard_map.100.refs_10_.refs_0_), channel_id=1, source_target_pairs={{8,0},{16,24},{9,1},{17,25},{10,2},{18,26},{11,3},{19,27},{12,4},{... | collective-permute-start | bytes 3538952 | tf_op jit(solution)/shard_map/ppermute | solution.py:197
  258.5 31.3 %collective-permute-start.18 = (bf16[3,768,256]{2,1,0:T(8,128)(2,1)S(1)}, bf16[3,768,256]{2,1,0:T(8,128)(2,1)S(1)}, u32[]{:S(2)}, u32[]{:S(2)}) collective-permute-start(bf16[3,768,256]{2,1,0:T(8,128)(2,1)S(1)} %shard_map.104.refs_10_.refs_0_), channel_id=1, source_target_pairs={{8,0},{16,24},{9,1},{17,25},{10,2},{18,26},{11,3},{19,27},{12,4},{... | collective-permute-start | bytes 3538952 | tf_op jit(solution)/shard_map/ppermute | solution.py:197
  283.3 32.2 %collective-permute-start.17 = (bf16[3,768,256]{2,1,0:T(8,128)(2,1)S(1)}, bf16[3,768,256]{2,1,0:T(8,128)(2,1)S(1)}, u32[]{:S(2)}, u32[]{:S(2)}) collective-permute-start(bf16[3,768,256]{2,1,0:T(8,128)(2,1)S(1)} %shard_map.108.refs_10_.refs_0_), channel_id=1, source_target_pairs={{8,0},{16,24},{9,1},{17,25},{10,2},{18,26},{11,3},{19,27},{12,4},{... | collective-permute-start | bytes 3538952 | tf_op jit(solution)/shard_map/ppermute | solution.py:197
  309.2 31.6 %collective-permute-start.22 = (bf16[3,768,256]{2,1,0:T(8,128)(2,1)S(1)}, bf16[3,768,256]{2,1,0:T(8,128)(2,1)S(1)}, u32[]{:S(2)}, u32[]{:S(2)}) collective-permute-start(bf16[3,768,256]{2,1,0:T(8,128)(2,1)S(1)} %shard_map.112.refs_10_.refs_0_), channel_id=1, source_target_pairs={{8,0},{16,24},{9,1},{17,25},{10,2},{18,26},{11,3},{19,27},{12,4},{... | collective-permute-start | bytes 3538952 | tf_op jit(solution)/shard_map/ppermute | solution.py:197
  334.5 31.8 %collective-permute-start.27 = (bf16[3,768,256]{2,1,0:T(8,128)(2,1)S(1)}, bf16[3,768,256]{2,1,0:T(8,128)(2,1)S(1)}, u32[]{:S(2)}, u32[]{:S(2)}) collective-permute-start(bf16[3,768,256]{2,1,0:T(8,128)(2,1)S(1)} %shard_map.116.refs_10_.refs_0_), channel_id=1, source_target_pairs={{8,0},{16,24},{9,1},{17,25},{10,2},{18,26},{11,3},{19,27},{12,4},{... | collective-permute-start | bytes 3538952 | tf_op jit(solution)/shard_map/ppermute | solution.py:197
  360.0 31.6 %collective-permute-start.30 = (bf16[3,768,256]{2,1,0:T(8,128)(2,1)S(1)}, bf16[3,768,256]{2,1,0:T(8,128)(2,1)S(1)}, u32[]{:S(2)}, u32[]{:S(2)}) collective-permute-start(bf16[3,768,256]{2,1,0:T(8,128)(2,1)S(1)} %shard_map.120.refs_10_.refs_0_), channel_id=1, source_target_pairs={{8,0},{16,24},{9,1},{17,25},{10,2},{18,26},{11,3},{19,27},{12,4},{... | collective-permute-start | bytes 3538952 | tf_op jit(solution)/shard_map/ppermute | solution.py:197
  385.3 31.7 %collective-permute-start.29 = (bf16[3,768,256]{2,1,0:T(8,128)(2,1)S(1)}, bf16[3,768,256]{2,1,0:T(8,128)(2,1)S(1)}, u32[]{:S(2)}, u32[]{:S(2)}) collective-permute-start(bf16[3,768,256]{2,1,0:T(8,128)(2,1)S(1)} %shard_map.124.refs_10_.refs_0_), channel_id=1, source_target_pairs={{8,0},{16,24},{9,1},{17,25},{10,2},{18,26},{11,3},{19,27},{12,4},{... | collective-permute-start | bytes 3538952 | tf_op jit(solution)/shard_map/ppermute | solution.py:197
  410.8 31.7 %collective-permute-start.34 = (bf16[3,768,256]{2,1,0:T(8,128)(2,1)S(1)}, bf16[3,768,256]{2,1,0:T(8,128)(2,1)S(1)}, u32[]{:S(2)}, u32[]{:S(2)}) collective-permute-start(bf16[3,768,256]{2,1,0:T(8,128)(2,1)S(1)} %shard_map.128.refs_10_.refs_0_), channel_id=1, source_target_pairs={{8,0},{16,24},{9,1},{17,25},{10,2},{18,26},{11,3},{19,27},{12,4},{... | collective-permute-start | bytes 3538952 | tf_op jit(solution)/shard_map/ppermute | solution.py:197
  436.2 31.7 %collective-permute-start.38 = (bf16[3,768,256]{2,1,0:T(8,128)(2,1)S(1)}, bf16[3,768,256]{2,1,0:T(8,128)(2,1)S(1)}, u32[]{:S(2)}, u32[]{:S(2)}) collective-permute-start(bf16[3,768,256]{2,1,0:T(8,128)(2,1)S(1)} %shard_map.132.refs_10_.refs_0_), channel_id=1, source_target_pairs={{8,0},{16,24},{9,1},{17,25},{10,2},{18,26},{11,3},{19,27},{12,4},{... | collective-permute-start | bytes 3538952 | tf_op jit(solution)/shard_map/ppermute | solution.py:197
  457.8 35.4 %collective-permute-start.41 = (bf16[3,768,256]{2,1,0:T(8,128)(2,1)S(1)}, bf16[3,768,256]{2,1,0:T(8,128)(2,1)S(1)}, u32[]{:S(2)}, u32[]{:S(2)}) collective-permute-start(bf16[3,768,256]{2,1,0:T(8,128)(2,1)S(1)} %shard_map.135.refs_10_.refs_0_), channel_id=1, source_target_pairs={{8,0},{16,24},{9,1},{17,25},{10,2},{18,26},{11,3},{19,27},{12,4},{... | collective-permute-start | bytes 3538952 | tf_op jit(solution)/shard_map/ppermute | solution.py:197
  478.5 37.8 %collective-permute-start.40 = (bf16[3,768,256]{2,1,0:T(8,128)(2,1)S(1)}, bf16[3,768,256]{2,1,0:T(8,128)(2,1)S(1)}, u32[]{:S(2)}, u32[]{:S(2)}) collective-permute-start(bf16[3,768,256]{2,1,0:T(8,128)(2,1)S(1)} %shard_map.137.refs_10_.refs_0_), channel_id=1, source_target_pairs={{8,0},{16,24},{9,1},{17,25},{10,2},{18,26},{11,3},{19,27},{12,4},{... | collective-permute-start | bytes 3538952 | tf_op jit(solution)/shard_map/ppermute | solution.py:197
  (37 other events, 667.6 us)
Sparse Core Ops, SparseCore 0:
  9.9 35.0 all-gather.2
  46.8 32.3 all-gather.4
  530.9 43.4 reduce-scatter.1

commit v2 on v1

--- a/solution.py
+++ b/solution.py
@@ -99,13 +99,62 @@
         run(mine_ref)
 
 
-def local(n, inputs, out_grad, w_gate, w_up, w_down):
+def bits_of(size):
+    bits = []
+    while 1 << len(bits) < size:
+        bits.append(len(bits))
+    return bits
+
+
+def flip(value, size, bit):
+    return lax.ppermute(value, "col", [(i, i ^ (1 << bit)) for i in range(size)])
+
+
+def gather_tokens(size, value, order):
+    index = lax.axis_index("col")
+    rows, model = value.shape
+    current = value
+    for bit in order:
+        got = flip(current, size, bit)
+        upper = ((index >> bit) & 1) == 1
+        low = jnp.where(upper, got, current)
+        high = jnp.where(upper, current, got)
+        current = jnp.stack([low, high])
+    held = list(reversed(order))
+    axes = [held.index(bit) for bit in sorted(order, reverse=True)]
+    current = current.transpose(axes + [len(axes), len(axes) + 1])
+    return current.reshape(size * rows, model)
+
+
+def scatter_tokens(size, value, order):
+    index = lax.axis_index("col")
+    tokens, model = value.shape
+    depth = len(order)
+    current = value.reshape((2,) * depth + (tokens // size, model))
+    for bit in order:
+        axis = depth - 1 - bit
+        mine = (index >> bit) & 1
+        kept = lax.dynamic_slice_in_dim(current, mine, 1, axis)
+        sent = lax.dynamic_slice_in_dim(current, 1 - mine, 1, axis).astype(BF)
+        current = kept + flip(sent, size, bit).astype(F32)
+    return current.reshape(tokens // size, model).astype(BF)
+
+
+def local(n, size, inputs, out_grad, w_gate, w_up, w_down):
     half = n // 2
     model, units = w_gate.shape
     width = divisor(units, 256, 128)
     count = units // width
-    in_all = lax.all_gather(inputs, "col", axis=0, tiled=True)
-    grad_all = lax.all_gather(out_grad, "col", axis=0, tiled=True)
+    bits = bits_of(size)
+    paired = 1 << len(bits) == size
+    up_order = bits[1:] + bits[:1]
+    down_order = bits[1:][::-1] + bits[:1]
+    if paired:
+        in_all = gather_tokens(size, inputs, up_order)
+        grad_all = gather_tokens(size, out_grad, down_order)
+    else:
+        in_all = lax.all_gather(inputs, "col", axis=0, tiled=True)
+        grad_all = lax.all_gather(out_grad, "col", axis=0, tiled=True)
     in_T = in_all.T
     tokens = in_all.shape[0]
     rows = divisor(tokens, 384, 256, 128)
@@ -166,8 +215,9 @@
             ins += list(state)
             specs += [acc, ANY, ANY, ANY]
             aliases = {6: 0, 7: 1, 8: 2, 9: 3}
-        ins.append(dep)
-        specs.append(ANY)
+        if fresh or dep is not state[3]:
+            ins.append(dep)
+            specs.append(ANY)
         return call(
             functools.partial(second_body, low, high, fresh),
             (model // depth,),
@@ -199,13 +249,23 @@
                 state = second(c, mine.pop(c), got.pop(c), state, last)
                 last = state[3]
     total, gw, gu, gd = state
-    grad_inputs = lax.psum_scatter(total.astype(BF), "col", scatter_dimension=0, tiled=True)
+    if paired:
+        middle = model // 2
+        grad_inputs = jnp.concatenate(
+            [
+                scatter_tokens(size, total[:, :middle], bits),
+                scatter_tokens(size, total[:, middle:], bits[:1] + bits[1:][::-1]),
+            ],
+            axis=1,
+        )
+    else:
+        grad_inputs = lax.psum_scatter(total.astype(BF), "col", scatter_dimension=0, tiled=True)
     return grad_inputs, gw, gu, gd
 
 
 def solution(mesh):
     return jax.shard_map(
-        functools.partial(local, mesh.shape["row"]),
+        functools.partial(local, mesh.shape["row"], mesh.shape["col"]),
         mesh=mesh,
         in_specs=(P("col", "row"), P("col", "row"), P("row", "col"), P("row", "col"), P("col", "row")),
         out_specs=(P("col", "row"), P("row", "col"), P("row", "col"), P("col", "row")),

time: 592 us -> 526 us (0.89)
  waiting for transfers between devices: 230 us -> 153 us
  starting transfers between devices: 76.4 us -> 97.7 us
  between operations: 15.1 us -> 2.16 us
  other arithmetic: 4.9 us -> 12.3 us
  local copies, waits for them, and re-layouts: 24.2 us -> 17 us
    all_gather x2 -> x0, waiting for transfers between devices: 70.5 us -> none  [the longest x1 36.2 us: local(): in_all = lax.all_gather(inputs, 'col', axis=0, tiled=True)]
    reduce_scatter x1 -> x0, waiting for transfers between devices: 43.6 us -> none  [local(): lax.psum_scatter(total.astype(BF), 'col', scatter_dimension=0, tiled=True)]
    ppermute x0 -> x12, waiting for transfers between devices: none -> 38.8 us  [flip(): return lax.ppermute(value, 'col', [(i, i ^ 1 << bit) for i in range(size)])]
    unnamed x33 -> x46, local copies, waits for them, and re-layouts: 19.6 us -> 5.51 us
    ppermute x0 -> x12, starting transfers between devices: none -> 13.6 us  [flip(): return lax.ppermute(value, 'col', [(i, i ^ 1 << bit) for i in range(size)])]
    another operation x0 -> x11, other arithmetic: none -> 6.56 us  [gather_tokens(): current = jnp.stack([low, high])]
    ppermute x14, starting transfers between devices: 45.7 us -> 52.3 us  [local(): got[t] = lax.ppermute(mine[t], 'row', perms[0])]
  transfers between devices with their start and end apart: 45 -> 54, of which waited for: 26 -> 34; matrix products, arithmetic and copies ran while one was open for 3% -> 3% of each run, Pallas kernels for 37% -> 42%
where the time goes in v2:
time: 526 us; the launch traced here: 518 us
  Pallas kernels  235 us (45%)
  waiting for transfers between devices  153 us (29%)
  starting transfers between devices  97.7 us (19%)
  local copies, waits for them, and re-layouts  17 us (3%)
  other arithmetic  12.3 us (2%)
    pallas_call x14, Pallas kernels, second(): call(functools.partial(second_body, low, high, fresh), (model // depth,),...  136 us
    pallas_call x14, Pallas kernels, first(): call(first_body, (tokens // rows,), [pl.BlockSpec((rows, model), lambda i...  68.5 us
    ppermute x28, waiting for transfers between devices, local(): got[c] = lax.ppermute(mine[c], 'row', perms[j + 1])  61.8 us
    ppermute x14, waiting for transfers between devices, local(): got[t] = lax.ppermute(mine[t], 'row', perms[0])  52.5 us
    ppermute x14, starting transfers between devices, local(): got[t] = lax.ppermute(mine[t], 'row', perms[0])  52.3 us
    ppermute x12, waiting for transfers between devices, flip(): return lax.ppermute(value, 'col', [(i, i ^ 1 << bit) for i in range(size)])  38.8 us
    ppermute x28, starting transfers between devices, local(): got[c] = lax.ppermute(mine[c], 'row', perms[j + 1])  31.9 us
    pallas_call x28, Pallas kernels, combine(): call(body, (tokens // rows * 2,), [spec, spec, ANY], spec, pack, (10 * sl...  31.2 us
  transfers between devices with their start and end apart: 54, of which 34 were waited for; matrix products, arithmetic and copies ran while one was open for 3% of the time, Pallas kernels for 42%

profile of v2, /device:TPU:0, one launch (start us, length us, event | category | flops | bytes accessed | tf_op | source)
XLA Modules:
  0.0 517.7 jit_solution(2534927791319144159)
XLA Ops:
  5.2 7.8 %collective-permute-done.3 = bf16[96,2048]{1,0:T(8,128)(2,1)S(1)} collective-permute-done((bf16[96,2048]{1,0:T(8,128)(2,1)}, bf16[96,2048]{1,0:T(8,128)(2,1)S(1)}, u32[]{:S(2)}, u32[]{:S(2)}) %collective-permute-start.3) | collective-permute-done | bytes 393248 | tf_op jit(solution)/shard_map/ppermute | solution.py:110
  17.6 15.3 %collective-permute-done.4 = bf16[2,96,2048]{2,1,0:T(8,128)(2,1)S(1)} collective-permute-done((bf16[2,96,2048]{2,1,0:T(8,128)(2,1)S(1)}, bf16[2,96,2048]{2,1,0:T(8,128)(2,1)S(1)}, u32[]{:S(2)}, u32[]{:S(2)}) %collective-permute-start.4) | collective-permute-done | bytes 786464 | tf_op jit(solution)/shard_map/ppermute | solution.py:110
  42.0 5.9 %shard_map.84.rest_0_.mine_ref = bf16[3,768,256]{2,1,0:T(8,128)(2,1)S(1)} custom-call(bf16[768,2048]{1,0:T(8,128)(2,1)S(1)} %bitcast.67, bf16[768,2048]{1,0:T(8,128)(2,1)S(1)} %bitcast.39, bf16[2048,3584]{1,0:T(8,128)(2,1)} %refs_4_.27, bf16[2048,3584]{1,0:T(8,128)(2,1)} %refs_5_.27, bf16[3584,2048]{1,0:T(8,128)(2,1)} %wd_ref.27), custom_call_target="tpu_custom_call" | custom-call | flops 2415919104 | bytes 10616832 | tf_op jit(solution)/shard_map/pallas_call | solution.py:175
  57.5 20.1 %collective-permute-done.7.got_ref = bf16[3,768,256]{2,1,0:T(8,128)(2,1)S(1)} collective-permute-done((bf16[3,768,256]{2,1,0:T(8,128)(2,1)S(1)}, bf16[3,768,256]{2,1,0:T(8,128)(2,1)S(1)}, u32[]{:S(2)}, u32[]{:S(2)}) %collective-permute-start.7) | collective-permute-done | bytes 1179680 | tf_op jit(solution)/shard_map/ppermute | solution.py:240
  83.7 7.2 %collective-permute-start.9 = (bf16[3,768,256]{2,1,0:T(8,128)(2,1)S(1)}, bf16[3,768,256]{2,1,0:T(8,128)(2,1)S(1)}, u32[]{:S(2)}, u32[]{:S(2)}) collective-permute-start(bf16[3,768,256]{2,1,0:T(8,128)(2,1)S(1)} %shard_map.87.dep_ref.mine_ref), channel_id=1, source_target_pairs={{0,8},{24,16},{1,9},{25,17},{2,10},{26,18},{3,11},{27,19},{4,12},{... | collective-permute-start | bytes 3538952 | tf_op jit(solution)/shard_map/ppermute | solution.py:240
  91.0 11.9 %collective-permute-done.6.got_ref = bf16[3,768,256]{2,1,0:T(8,128)(2,1)S(1)} collective-permute-done((bf16[3,768,256]{2,1,0:T(8,128)(2,1)S(1)}, bf16[3,768,256]{2,1,0:T(8,128)(2,1)S(1)}, u32[]{:S(2)}, u32[]{:S(2)}) %collective-permute-start.6) | collective-permute-done | bytes 1179680 | tf_op jit(solution)/shard_map/ppermute | solution.py:240
  113.2 9.2 %collective-permute-start.14 = (bf16[3,768,256]{2,1,0:T(8,128)(2,1)}, bf16[3,768,256]{2,1,0:T(8,128)(2,1)}, u32[]{:S(2)}, u32[]{:S(2)}) collective-permute-start(bf16[3,768,256]{2,1,0:T(8,128)(2,1)} %shard_map.90.dep_ref.mine_ref), channel_id=1, source_target_pairs={{0,8},{24,16},{1,9},{25,17},{2,10},{26,18},{3,11},{27,19},{4,12},{... | collective-permute-start | bytes 3538952 | tf_op jit(solution)/shard_map/ppermute | solution.py:240
  142.0 8.8 %shard_map.93 = (f32[768,2048]{1,0:T(8,128)}, bf16[2048,3584]{1,0:T(8,128)(2,1)}, bf16[2048,3584]{1,0:T(8,128)(2,1)}, bf16[3584,2048]{1,0:T(8,128)(2,1)}) custom-call(bf16[3,768,256]{2,1,0:T(8,128)(2,1)} %shard_map.89.rest_0_.refs_0_, bf16[3,768,256]{2,1,0:T(8,128)(2,1)} %collective-permute-done.12.refs_1_, bf16[2048,768]{1,0:T(8,128)(2,1)S(1)} %bitcast.82, ...), custom_call_target="tpu_custom_call" | custom-call | flops 4026531840 | bytes 26476544 | tf_op jit(solution)/shard_map/pallas_call | solution.py:221
  155.6 7.3 %collective-permute-start.18 = (bf16[3,768,256]{2,1,0:T(8,128)(2,1)S(1)}, bf16[3,768,256]{2,1,0:T(8,128)(2,1)S(1)}, u32[]{:S(2)}, u32[]{:S(2)}) collective-permute-start(bf16[3,768,256]{2,1,0:T(8,128)(2,1)S(1)} %shard_map.94.dep_ref.mine_ref), channel_id=1, source_target_pairs={{0,8},{24,16},{1,9},{25,17},{2,10},{26,18},{3,11},{27,19},{4,12},{... | collective-permute-start | bytes 3538952 | tf_op jit(solution)/shard_map/ppermute | solution.py:240
  170.4 10.3 %shard_map.97 = (f32[768,2048]{1,0:T(8,128)}, bf16[2048,3584]{1,0:T(8,128)(2,1)}, bf16[2048,3584]{1,0:T(8,128)(2,1)}, bf16[3584,2048]{1,0:T(8,128)(2,1)}) custom-call(bf16[3,768,256]{2,1,0:T(8,128)(2,1)} %shard_map.92.refs_6_.refs_0_, ...), custom_call_target="tpu_custom_call", output_to_operand_aliasing={{0}: (6, {}), {1}: (7, {}), {2}: (8, {}), {3}: (9, {})} | custom-call | flops 4026531840 | bytes 26476544 | tf_op jit(solution)/shard_map/pallas_call | solution.py:221
  198.3 9.9 %shard_map.101 = (f32[768,2048]{1,0:T(8,128)}, bf16[2048,3584]{1,0:T(8,128)(2,1)}, bf16[2048,3584]{1,0:T(8,128)(2,1)}, bf16[3584,2048]{1,0:T(8,128)(2,1)}) custom-call(bf16[3,768,256]{2,1,0:T(8,128)(2,1)S(1)} %shard_map.96.refs_10_.refs_0_, ...), custom_call_target="tpu_custom_call", output_to_operand_aliasing={{0}: (6, {}), {1}: (7, {}), {2}: (8, {}), {3}: (9, {})} | custom-call | flops 4026531840 | bytes 26476544 | tf_op jit(solution)/shard_map/pallas_call | solution.py:221
  224.4 9.6 %shard_map.105 = (f32[768,2048]{1,0:T(8,128)}, bf16[2048,3584]{1,0:T(8,128)(2,1)}, bf16[2048,3584]{1,0:T(8,128)(2,1)}, bf16[3584,2048]{1,0:T(8,128)(2,1)}) custom-call(bf16[3,768,256]{2,1,0:T(8,128)(2,1)S(1)} %shard_map.100.refs_10_.refs_0_, ...), custom_call_target="tpu_custom_call", output_to_operand_aliasing={{0}: (6, {}), {1}: (7, {}), {2}: (8, {}), {3}: (9, {})} | custom-call | flops 4026531840 | bytes 26476544 | tf_op jit(solution)/shard_map/pallas_call | solution.py:221
  249.3 9.6 %shard_map.109 = (f32[768,2048]{1,0:T(8,128)}, bf16[2048,3584]{1,0:T(8,128)(2,1)}, bf16[2048,3584]{1,0:T(8,128)(2,1)}, bf16[3584,2048]{1,0:T(8,128)(2,1)}) custom-call(bf16[3,768,256]{2,1,0:T(8,128)(2,1)S(1)} %shard_map.104.refs_10_.refs_0_, ...), custom_call_target="tpu_custom_call", output_to_operand_aliasing={{0}: (6, {}), {1}: (7, {}), {2}: (8, {}), {3}: (9, {})} | custom-call | flops 4026531840 | bytes 26476544 | tf_op jit(solution)/shard_map/pallas_call | solution.py:221
  275.3 9.6 %shard_map.113 = (f32[768,2048]{1,0:T(8,128)}, bf16[2048,3584]{1,0:T(8,128)(2,1)}, bf16[2048,3584]{1,0:T(8,128)(2,1)}, bf16[3584,2048]{1,0:T(8,128)(2,1)}) custom-call(bf16[3,768,256]{2,1,0:T(8,128)(2,1)S(1)} %shard_map.108.refs_10_.refs_0_, ...), custom_call_target="tpu_custom_call", output_to_operand_aliasing={{0}: (6, {}), {1}: (7, {}), {2}: (8, {}), {3}: (9, {})} | custom-call | flops 4026531840 | bytes 26476544 | tf_op jit(solution)/shard_map/pallas_call | solution.py:221
  300.6 9.6 %shard_map.117 = (f32[768,2048]{1,0:T(8,128)}, bf16[2048,3584]{1,0:T(8,128)(2,1)}, bf16[2048,3584]{1,0:T(8,128)(2,1)}, bf16[3584,2048]{1,0:T(8,128)(2,1)}) custom-call(bf16[3,768,256]{2,1,0:T(8,128)(2,1)S(1)} %shard_map.112.refs_10_.refs_0_, ...), custom_call_target="tpu_custom_call", output_to_operand_aliasing={{0}: (6, {}), {1}: (7, {}), {2}: (8, {}), {3}: (9, {})} | custom-call | flops 4026531840 | bytes 26476544 | tf_op jit(solution)/shard_map/pallas_call | solution.py:221
  325.9 9.6 %shard_map.121 = (f32[768,2048]{1,0:T(8,128)}, bf16[2048,3584]{1,0:T(8,128)(2,1)}, bf16[2048,3584]{1,0:T(8,128)(2,1)}, bf16[3584,2048]{1,0:T(8,128)(2,1)}) custom-call(bf16[3,768,256]{2,1,0:T(8,128)(2,1)S(1)} %shard_map.116.refs_10_.refs_0_, ...), custom_call_target="tpu_custom_call", output_to_operand_aliasing={{0}: (6, {}), {1}: (7, {}), {2}: (8, {}), {3}: (9, {})} | custom-call | flops 4026531840 | bytes 26476544 | tf_op jit(solution)/shard_map/pallas_call | solution.py:221
  351.3 9.6 %shard_map.125 = (f32[768,2048]{1,0:T(8,128)}, bf16[2048,3584]{1,0:T(8,128)(2,1)}, bf16[2048,3584]{1,0:T(8,128)(2,1)}, bf16[3584,2048]{1,0:T(8,128)(2,1)}) custom-call(bf16[3,768,256]{2,1,0:T(8,128)(2,1)S(1)} %shard_map.120.refs_10_.refs_0_, ...), custom_call_target="tpu_custom_call", output_to_operand_aliasing={{0}: (6, {}), {1}: (7, {}), {2}: (8, {}), {3}: (9, {})} | custom-call | flops 4026531840 | bytes 26476544 | tf_op jit(solution)/shard_map/pallas_call | solution.py:221
  376.6 9.6 %shard_map.129 = (f32[768,2048]{1,0:T(8,128)}, bf16[2048,3584]{1,0:T(8,128)(2,1)}, bf16[2048,3584]{1,0:T(8,128)(2,1)}, bf16[3584,2048]{1,0:T(8,128)(2,1)}) custom-call(bf16[3,768,256]{2,1,0:T(8,128)(2,1)S(1)} %shard_map.124.refs_10_.refs_0_, ...), custom_call_target="tpu_custom_call", output_to_operand_aliasing={{0}: (6, {}), {1}: (7, {}), {2}: (8, {}), {3}: (9, {})} | custom-call | flops 4026531840 | bytes 26476544 | tf_op jit(solution)/shard_map/pallas_call | solution.py:221
  401.9 9.6 %shard_map.133 = (f32[768,2048]{1,0:T(8,128)}, bf16[2048,3584]{1,0:T(8,128)(2,1)}, bf16[2048,3584]{1,0:T(8,128)(2,1)}, bf16[3584,2048]{1,0:T(8,128)(2,1)}) custom-call(bf16[3,768,256]{2,1,0:T(8,128)(2,1)S(1)} %shard_map.128.refs_10_.refs_0_, ...), custom_call_target="tpu_custom_call", output_to_operand_aliasing={{0}: (6, {}), {1}: (7, {}), {2}: (8, {}), {3}: (9, {})} | custom-call | flops 4026531840 | bytes 26476544 | tf_op jit(solution)/shard_map/pallas_call | solution.py:221
  426.3 9.6 %shard_map.136 = (f32[768,2048]{1,0:T(8,128)}, bf16[2048,3584]{1,0:T(8,128)(2,1)}, bf16[2048,3584]{1,0:T(8,128)(2,1)}, bf16[3584,2048]{1,0:T(8,128)(2,1)}) custom-call(bf16[3,768,256]{2,1,0:T(8,128)(2,1)S(1)} %shard_map.132.refs_10_.refs_0_, ...), custom_call_target="tpu_custom_call", output_to_operand_aliasing={{0}: (6, {}), {1}: (7, {}), {2}: (8, {}), {3}: (9, {})} | custom-call | flops 4026531840 | bytes 26476544 | tf_op jit(solution)/shard_map/pallas_call | solution.py:221
  439.5 11.5 %collective-permute-done.47.refs_1_ = bf16[3,768,256]{2,1,0:T(8,128)(2,1)} collective-permute-done((bf16[3,768,256]{2,1,0:T(8,128)(2,1)}, bf16[3,768,256]{2,1,0:T(8,128)(2,1)}, u32[]{:S(2)}, u32[]{:S(2)}) %collective-permute-start.47) | collective-permute-done | bytes 1179680 | tf_op jit(solution)/shard_map/ppermute | solution.py:247
  452.9 10.3 %shard_map.138 = (f32[768,2048]{1,0:T(8,128)}, bf16[2048,3584]{1,0:T(8,128)(2,1)}, bf16[2048,3584]{1,0:T(8,128)(2,1)}, bf16[3584,2048]{1,0:T(8,128)(2,1)}) custom-call(bf16[3,768,256]{2,1,0:T(8,128)(2,1)} %shard_map.135.refs_10_.refs_0_, ...), custom_call_target="tpu_custom_call", output_to_operand_aliasing={{0}: (6, {}), {1}: (7, {}), {2}: (8, {}), {3}: (9, {})} | custom-call | flops 4026531840 | bytes 26476544 | tf_op jit(solution)/shard_map/pallas_call | solution.py:221
  463.2 11.8 %collective-permute-done.46.refs_1_ = bf16[3,768,256]{2,1,0:T(8,128)(2,1)} collective-permute-done((bf16[3,768,256]{2,1,0:T(8,128)(2,1)}, bf16[3,768,256]{2,1,0:T(8,128)(2,1)}, u32[]{:S(2)}, u32[]{:S(2)}) %collective-permute-start.46) | collective-permute-done | bytes 1179680 | tf_op jit(solution)/shard_map/ppermute | solution.py:247
  475.0 10.3 %shard_map.139 = (f32[768,2048]{1,0:T(8,128)}, bf16[2048,3584]{1,0:T(8,128)(2,1)}, bf16[2048,3584]{1,0:T(8,128)(2,1)}, bf16[3584,2048]{1,0:T(8,128)(2,1)}) custom-call(bf16[3,768,256]{2,1,0:T(8,128)(2,1)} %shard_map.137.refs_10_.refs_0_, ...), custom_call_target="tpu_custom_call", output_to_operand_aliasing={{0}: (6, {}), {1}: (7, {}), {2}: (8, {}), {3}: (9, {})} | custom-call | flops 4026531840 | bytes 26476544 | tf_op jit(solution)/shard_map/pallas_call | solution.py:221
  (214 shorter events, 271.8 us)
Async XLA Ops:
  47.9 29.7 %collective-permute-start.7 = (bf16[3,768,256]{2,1,0:T(8,128)(2,1)S(1)}, bf16[3,768,256]{2,1,0:T(8,128)(2,1)S(1)}, u32[]{:S(2)}, u32[]{:S(2)}) collective-permute-start(bf16[3,768,256]{2,1,0:T(8,128)(2,1)S(1)} %shard_map.84.rest_0_.mine_ref), channel_id=1, source_target_pairs={{0,8},{24,16},{1,9},{25,17},{2,10},{26,18},{3,11},{27,19},{4,12},{... | collective-permute-start | bytes 3538952 | tf_op jit(solution)/shard_map/ppermute | solution.py:240
  56.2 46.7 %collective-permute-start.6 = (bf16[3,768,256]{2,1,0:T(8,128)(2,1)S(1)}, bf16[3,768,256]{2,1,0:T(8,128)(2,1)S(1)}, u32[]{:S(2)}, u32[]{:S(2)}) collective-permute-start(bf16[3,768,256]{2,1,0:T(8,128)(2,1)S(1)} %shard_map.85.dep_ref.mine_ref), channel_id=1, source_target_pairs={{0,8},{24,16},{1,9},{25,17},{2,10},{26,18},{3,11},{27,19},{4,12},{... | collective-permute-start | bytes 3538952 | tf_op jit(solution)/shard_map/ppermute | solution.py:240
  83.7 44.4 %collective-permute-start.9 = (bf16[3,768,256]{2,1,0:T(8,128)(2,1)S(1)}, bf16[3,768,256]{2,1,0:T(8,128)(2,1)S(1)}, u32[]{:S(2)}, u32[]{:S(2)}) collective-permute-start(bf16[3,768,256]{2,1,0:T(8,128)(2,1)S(1)} %shard_map.87.dep_ref.mine_ref), channel_id=1, source_target_pairs={{0,8},{24,16},{1,9},{25,17},{2,10},{26,18},{3,11},{27,19},{4,12},{... | collective-permute-start | bytes 3538952 | tf_op jit(solution)/shard_map/ppermute | solution.py:240
  106.3 33.8 %collective-permute-start.12 = (bf16[3,768,256]{2,1,0:T(8,128)(2,1)}, bf16[3,768,256]{2,1,0:T(8,128)(2,1)}, u32[]{:S(2)}, u32[]{:S(2)}) collective-permute-start(bf16[3,768,256]{2,1,0:T(8,128)(2,1)} %shard_map.89.rest_0_.refs_0_), channel_id=1, source_target_pairs={{8,0},{16,24},{9,1},{17,25},{10,2},{18,26},{11,3},{19,27},{12,4},{... | collective-permute-start | bytes 3538952 | tf_op jit(solution)/shard_map/ppermute | solution.py:247
  113.2 49.7 %collective-permute-start.14 = (bf16[3,768,256]{2,1,0:T(8,128)(2,1)}, bf16[3,768,256]{2,1,0:T(8,128)(2,1)}, u32[]{:S(2)}, u32[]{:S(2)}) collective-permute-start(bf16[3,768,256]{2,1,0:T(8,128)(2,1)} %shard_map.90.dep_ref.mine_ref), channel_id=1, source_target_pairs={{0,8},{24,16},{1,9},{25,17},{2,10},{26,18},{3,11},{27,19},{4,12},{... | collective-permute-start | bytes 3538952 | tf_op jit(solution)/shard_map/ppermute | solution.py:240
  130.0 36.3 %collective-permute-start.13 = (bf16[3,768,256]{2,1,0:T(8,128)(2,1)}, bf16[3,768,256]{2,1,0:T(8,128)(2,1)}, u32[]{:S(2)}, u32[]{:S(2)}) collective-permute-start(bf16[3,768,256]{2,1,0:T(8,128)(2,1)} %shard_map.91.dep_ref.mine_ref), channel_id=1, source_target_pairs={{8,16},{16,8},{9,17},{17,9},{10,18},{18,10},{11,19},{19,11},{12,20... | collective-permute-start | bytes 3538952 | tf_op jit(solution)/shard_map/ppermute | solution.py:247
  133.8 36.6 %collective-permute-start.11 = (bf16[3,768,256]{2,1,0:T(8,128)(2,1)}, bf16[3,768,256]{2,1,0:T(8,128)(2,1)}, u32[]{:S(2)}, u32[]{:S(2)}) collective-permute-start(bf16[3,768,256]{2,1,0:T(8,128)(2,1)} %shard_map.92.refs_6_.refs_0_), channel_id=1, source_target_pairs={{8,0},{16,24},{9,1},{17,25},{10,2},{18,26},{11,3},{19,27},{12,4},{... | collective-permute-start | bytes 3538952 | tf_op jit(solution)/shard_map/ppermute | solution.py:247
  155.6 35.5 %collective-permute-start.18 = (bf16[3,768,256]{2,1,0:T(8,128)(2,1)S(1)}, bf16[3,768,256]{2,1,0:T(8,128)(2,1)S(1)}, u32[]{:S(2)}, u32[]{:S(2)}) collective-permute-start(bf16[3,768,256]{2,1,0:T(8,128)(2,1)S(1)} %shard_map.94.dep_ref.mine_ref), channel_id=1, source_target_pairs={{0,8},{24,16},{1,9},{25,17},{2,10},{26,18},{3,11},{27,19},{4,12},{... | collective-permute-start | bytes 3538952 | tf_op jit(solution)/shard_map/ppermute | solution.py:240
  169.1 29.1 %collective-permute-start.16 = (bf16[3,768,256]{2,1,0:T(8,128)(2,1)S(1)}, bf16[3,768,256]{2,1,0:T(8,128)(2,1)}, u32[]{:S(2)}, u32[]{:S(2)}) collective-permute-start(bf16[3,768,256]{2,1,0:T(8,128)(2,1)S(1)} %shard_map.96.refs_10_.refs_0_), channel_id=1, source_target_pairs={{8,0},{16,24},{9,1},{17,25},{10,2},{18,26},{11,3},{19,27},{12,4},{... | collective-permute-start | bytes 3538952 | tf_op jit(solution)/shard_map/ppermute | solution.py:247
  185.5 31.2 %collective-permute-start.15 = (bf16[3,768,256]{2,1,0:T(8,128)(2,1)S(1)}, bf16[3,768,256]{2,1,0:T(8,128)(2,1)S(1)}, u32[]{:S(2)}, u32[]{:S(2)}) collective-permute-start(bf16[3,768,256]{2,1,0:T(8,128)(2,1)S(1)} %shard_map.98.dep_ref.mine_ref), channel_id=1, source_target_pairs={{0,8},{24,16},{1,9},{25,17},{2,10},{26,18},{3,11},{27,19},{4,12},{... | collective-permute-start | bytes 3538952 | tf_op jit(solution)/shard_map/ppermute | solution.py:240
  193.6 30.8 %collective-permute-start.21 = (bf16[3,768,256]{2,1,0:T(8,128)(2,1)S(1)}, bf16[3,768,256]{2,1,0:T(8,128)(2,1)S(1)}, u32[]{:S(2)}, u32[]{:S(2)}) collective-permute-start(bf16[3,768,256]{2,1,0:T(8,128)(2,1)S(1)} %shard_map.100.refs_10_.refs_0_), channel_id=1, source_target_pairs={{8,0},{16,24},{9,1},{17,25},{10,2},{18,26},{11,3},{19,27},{12,4},{... | collective-permute-start | bytes 3538952 | tf_op jit(solution)/shard_map/ppermute | solution.py:247
  212.9 29.0 %collective-permute-start.20 = (bf16[3,768,256]{2,1,0:T(8,128)(2,1)S(1)}, bf16[3,768,256]{2,1,0:T(8,128)(2,1)S(1)}, u32[]{:S(2)}, u32[]{:S(2)}) collective-permute-start(bf16[3,768,256]{2,1,0:T(8,128)(2,1)S(1)} %shard_map.102.dep_ref.mine_ref), channel_id=1, source_target_pairs={{0,8},{24,16},{1,9},{25,17},{2,10},{26,18},{3,11},{27,19},{4,12},{... | collective-permute-start | bytes 3538952 | tf_op jit(solution)/shard_map/ppermute | solution.py:240
  219.1 30.2 %collective-permute-start.24 = (bf16[3,768,256]{2,1,0:T(8,128)(2,1)S(1)}, bf16[3,768,256]{2,1,0:T(8,128)(2,1)S(1)}, u32[]{:S(2)}, u32[]{:S(2)}) collective-permute-start(bf16[3,768,256]{2,1,0:T(8,128)(2,1)S(1)} %shard_map.104.refs_10_.refs_0_), channel_id=1, source_target_pairs={{8,0},{16,24},{9,1},{17,25},{10,2},{18,26},{11,3},{19,27},{12,4},{... | collective-permute-start | bytes 3538952 | tf_op jit(solution)/shard_map/ppermute | solution.py:247
  238.7 29.1 %collective-permute-start.26 = (bf16[3,768,256]{2,1,0:T(8,128)(2,1)S(1)}, bf16[3,768,256]{2,1,0:T(8,128)(2,1)S(1)}, u32[]{:S(2)}, u32[]{:S(2)}) collective-permute-start(bf16[3,768,256]{2,1,0:T(8,128)(2,1)S(1)} %shard_map.106.dep_ref.mine_ref), channel_id=1, source_target_pairs={{0,8},{24,16},{1,9},{25,17},{2,10},{26,18},{3,11},{27,19},{4,12},{... | collective-permute-start | bytes 3538952 | tf_op jit(solution)/shard_map/ppermute | solution.py:240
  244.4 31.0 %collective-permute-start.23 = (bf16[3,768,256]{2,1,0:T(8,128)(2,1)S(1)}, bf16[3,768,256]{2,1,0:T(8,128)(2,1)S(1)}, u32[]{:S(2)}, u32[]{:S(2)}) collective-permute-start(bf16[3,768,256]{2,1,0:T(8,128)(2,1)S(1)} %shard_map.108.refs_10_.refs_0_), channel_id=1, source_target_pairs={{8,0},{16,24},{9,1},{17,25},{10,2},{18,26},{11,3},{19,27},{12,4},{... | collective-permute-start | bytes 3538952 | tf_op jit(solution)/shard_map/ppermute | solution.py:247
  263.6 29.4 %collective-permute-start.30 = (bf16[3,768,256]{2,1,0:T(8,128)(2,1)S(1)}, bf16[3,768,256]{2,1,0:T(8,128)(2,1)S(1)}, u32[]{:S(2)}, u32[]{:S(2)}) collective-permute-start(bf16[3,768,256]{2,1,0:T(8,128)(2,1)S(1)} %shard_map.110.dep_ref.mine_ref), channel_id=1, source_target_pairs={{0,8},{24,16},{1,9},{25,17},{2,10},{26,18},{3,11},{27,19},{4,12},{... | collective-permute-start | bytes 3538952 | tf_op jit(solution)/shard_map/ppermute | solution.py:240
  270.2 30.4 %collective-permute-start.28 = (bf16[3,768,256]{2,1,0:T(8,128)(2,1)S(1)}, bf16[3,768,256]{2,1,0:T(8,128)(2,1)S(1)}, u32[]{:S(2)}, u32[]{:S(2)}) collective-permute-start(bf16[3,768,256]{2,1,0:T(8,128)(2,1)S(1)} %shard_map.112.refs_10_.refs_0_), channel_id=1, source_target_pairs={{8,0},{16,24},{9,1},{17,25},{10,2},{18,26},{11,3},{19,27},{12,4},{... | collective-permute-start | bytes 3538952 | tf_op jit(solution)/shard_map/ppermute | solution.py:247
  295.5 30.4 %collective-permute-start.33 = (bf16[3,768,256]{2,1,0:T(8,128)(2,1)S(1)}, bf16[3,768,256]{2,1,0:T(8,128)(2,1)S(1)}, u32[]{:S(2)}, u32[]{:S(2)}) collective-permute-start(bf16[3,768,256]{2,1,0:T(8,128)(2,1)S(1)} %shard_map.116.refs_10_.refs_0_), channel_id=1, source_target_pairs={{8,0},{16,24},{9,1},{17,25},{10,2},{18,26},{11,3},{19,27},{12,4},{... | collective-permute-start | bytes 3538952 | tf_op jit(solution)/shard_map/ppermute | solution.py:247
  320.8 30.5 %collective-permute-start.36 = (bf16[3,768,256]{2,1,0:T(8,128)(2,1)S(1)}, bf16[3,768,256]{2,1,0:T(8,128)(2,1)S(1)}, u32[]{:S(2)}, u32[]{:S(2)}) collective-permute-start(bf16[3,768,256]{2,1,0:T(8,128)(2,1)S(1)} %shard_map.120.refs_10_.refs_0_), channel_id=1, source_target_pairs={{8,0},{16,24},{9,1},{17,25},{10,2},{18,26},{11,3},{19,27},{12,4},{... | collective-permute-start | bytes 3538952 | tf_op jit(solution)/shard_map/ppermute | solution.py:247
  346.2 30.4 %collective-permute-start.35 = (bf16[3,768,256]{2,1,0:T(8,128)(2,1)S(1)}, bf16[3,768,256]{2,1,0:T(8,128)(2,1)S(1)}, u32[]{:S(2)}, u32[]{:S(2)}) collective-permute-start(bf16[3,768,256]{2,1,0:T(8,128)(2,1)S(1)} %shard_map.124.refs_10_.refs_0_), channel_id=1, source_target_pairs={{8,0},{16,24},{9,1},{17,25},{10,2},{18,26},{11,3},{19,27},{12,4},{... | collective-permute-start | bytes 3538952 | tf_op jit(solution)/shard_map/ppermute | solution.py:247
  371.5 30.4 %collective-permute-start.40 = (bf16[3,768,256]{2,1,0:T(8,128)(2,1)S(1)}, bf16[3,768,256]{2,1,0:T(8,128)(2,1)S(1)}, u32[]{:S(2)}, u32[]{:S(2)}) collective-permute-start(bf16[3,768,256]{2,1,0:T(8,128)(2,1)S(1)} %shard_map.128.refs_10_.refs_0_), channel_id=1, source_target_pairs={{8,0},{16,24},{9,1},{17,25},{10,2},{18,26},{11,3},{19,27},{12,4},{... | collective-permute-start | bytes 3538952 | tf_op jit(solution)/shard_map/ppermute | solution.py:247
  396.8 29.5 %collective-permute-start.44 = (bf16[3,768,256]{2,1,0:T(8,128)(2,1)S(1)}, bf16[3,768,256]{2,1,0:T(8,128)(2,1)S(1)}, u32[]{:S(2)}, u32[]{:S(2)}) collective-permute-start(bf16[3,768,256]{2,1,0:T(8,128)(2,1)S(1)} %shard_map.132.refs_10_.refs_0_), channel_id=1, source_target_pairs={{8,0},{16,24},{9,1},{17,25},{10,2},{18,26},{11,3},{19,27},{12,4},{... | collective-permute-start | bytes 3538952 | tf_op jit(solution)/shard_map/ppermute | solution.py:247
  419.7 31.3 %collective-permute-start.47 = (bf16[3,768,256]{2,1,0:T(8,128)(2,1)}, bf16[3,768,256]{2,1,0:T(8,128)(2,1)}, u32[]{:S(2)}, u32[]{:S(2)}) collective-permute-start(bf16[3,768,256]{2,1,0:T(8,128)(2,1)} %shard_map.135.refs_10_.refs_0_), channel_id=1, source_target_pairs={{8,0},{16,24},{9,1},{17,25},{10,2},{18,26},{11,3},{19,27},{12,4},{... | collective-permute-start | bytes 3538952 | tf_op jit(solution)/shard_map/ppermute | solution.py:247
  438.0 37.0 %collective-permute-start.46 = (bf16[3,768,256]{2,1,0:T(8,128)(2,1)}, bf16[3,768,256]{2,1,0:T(8,128)(2,1)}, u32[]{:S(2)}, u32[]{:S(2)}) collective-permute-start(bf16[3,768,256]{2,1,0:T(8,128)(2,1)} %shard_map.137.refs_10_.refs_0_), channel_id=1, source_target_pairs={{8,0},{16,24},{9,1},{17,25},{10,2},{18,26},{11,3},{19,27},{12,4},{... | collective-permute-start | bytes 3538952 | tf_op jit(solution)/shard_map/ppermute | solution.py:247
  (53 other events, 764.8 us)
